TPU v7x, 32 devices: a whole 2x2x4 slice. The times are simulated.
32 devices in a mesh: groups: 2 (over y), row: 8 (over z, x), col: 2 (over core).
Axes of the slice: x: 2, y: 2, z: 4, core: 2. Of those that a mesh axis runs over, the one named last changes fastest.
Arguments:
- tokens: bfloat16 [768, 8192], P(('groups', 'col'), 'row'), parts along dimension 0, may hold values from -6 to 6
- gate_up_blocks: bfloat16 [2, 2, 2048, 128, 128], P(None, 'col', 'row'), may hold values from -0.125 to 0.125
- gate_up_index: int32 [2, 2048], P('col', 'row'), may hold values from 0 to 511, as said below
- gate_up_count: int32 [2, 8], P('col', 'row'), may hold values from 1 to 256, as said below
- down_blocks: bfloat16 [2, 2048, 128, 128], P('col', 'row'), may hold values from -0.09375 to 0.09375
- down_index: int32 [2, 2048], P('col', 'row'), may hold values from 0 to 511, as said below
- down_count: int32 [2, 8], P('col', 'row'), may hold values from 1 to 256, as said below
- grad_out: bfloat16 [768, 8192], P(('groups', 'col'), 'row'), parts along dimension 0, may hold values from -6 to 6
Outputs:
- output: bfloat16 [768, 8192], P(('groups', 'col'), 'row'), parts along dimension 0
- grad_in: bfloat16 [768, 8192], P(('groups', 'col'), 'row'), parts along dimension 0
- grad_gate_up: float32 [2, 4, 2048, 128, 128], P(None, ('groups', 'col'), 'row'), parts along dimension 1
- grad_down: float32 [4, 2048, 128, 128], P(('groups', 'col'), 'row'), parts along dimension 0
There are 2 independent parts, one for each index of `groups`. A program takes and returns all parts, laid end to end along the dimension named above; an argument that names none is the same for every part. Nothing has to cross between parts.
Inputs may be any that keep to these rules, and one draw needn't show every extreme that they name: `gate_up_index`: within each panel the 256 positions are distinct. `gate_up_count`: some panel has all 256 slots live. `down_index`: within each panel the 256 positions are distinct. `down_count`: some panel has all 256 slots live.
All inputs are finite; a program needn't handle non-finite values.
Results may differ from a plain program's by a relative error of at most 0.005.
Values may be sent and summed in bfloat16 or wider, within the bound.
A program may use at most 448 MiB of HBM per device.

v0:
```python
import jax
import jax.numpy as jnp
from jax import lax
from jax.sharding import PartitionSpec as P

FFW = 16384


def place_terms(terms, live, targets, count):
    masked = terms * live.reshape((live.shape[0],) + (1,) * (terms.ndim - 1))
    return jax.ops.segment_sum(masked, targets, num_segments=count)


def per_device(
    tokens,
    gate_up_blocks,
    gate_up_index,
    gate_up_count,
    down_blocks,
    down_index,
    down_count,
    grad_out,
):
    n_row = lax.axis_size("row")
    n_col = lax.axis_size("col")
    block_size = gate_up_blocks.shape[-1]
    slot_count = gate_up_blocks.shape[2]
    full_width = tokens.shape[1] * n_row
    half_rows = full_width // (n_col * block_size)
    panel_cols = FFW // (n_row * block_size)
    d_blocks = full_width // block_size
    tok_rows = tokens.shape[0]
    slot_range = jnp.arange(slot_count, dtype=jnp.int32)
    halves = jnp.arange(n_col, dtype=jnp.int32)[:, None]
    gathered = lax.all_gather(tokens, "row", axis=1, tiled=True)
    gu_all, gu_index, gu_count = (
        lax.all_gather(gate_up_blocks, "col", axis=1, tiled=True),
        lax.all_gather(gate_up_index, "col", axis=0, tiled=True),
        lax.all_gather(gate_up_count, "col", axis=0, tiled=True),
    )
    live_gu = (slot_range[None, :] < gu_count).reshape(-1).astype(jnp.float32)
    d_of_gu = (halves * half_rows + gu_index // panel_cols).reshape(-1)
    f_of_gu = (gu_index % panel_cols).reshape(-1)
    w_gu = gu_all.reshape(2, n_col * slot_count, block_size, block_size)
    x_sel = jnp.take(gathered.reshape(tok_rows, d_blocks, block_size), d_of_gu, axis=1)
    term_blocks = jnp.einsum("tsk,gskn->sgtn", x_sel, w_gu, preferred_element_type=jnp.float32)
    placed_gu = place_terms(term_blocks, live_gu, f_of_gu, panel_cols)
    gate_up = placed_gu.transpose(1, 2, 0, 3).reshape(2, tok_rows, panel_cols * block_size)
    sigmoid = jax.nn.sigmoid(gate_up[0])
    act_f = gate_up[0] * sigmoid
    slope_term = sigmoid * (1.0 + gate_up[0] * (1.0 - sigmoid))
    hidden = (act_f * gate_up[1]).astype(jnp.bfloat16)
    dn_all, dn_index, dn_count = (
        lax.all_gather(down_blocks, "col", axis=0, tiled=True),
        lax.all_gather(down_index, "col", axis=0, tiled=True),
        lax.all_gather(down_count, "col", axis=0, tiled=True),
    )
    live_dn = (slot_range[None, :] < dn_count).reshape(-1).astype(jnp.float32)
    f_of_dn = (dn_index // half_rows).reshape(-1)
    d_of_dn = (halves * half_rows + dn_index % half_rows).reshape(-1)
    w_dn = dn_all.reshape(n_col * slot_count, block_size, block_size)
    h_sel = jnp.take(hidden.reshape(tok_rows, panel_cols, block_size), f_of_dn, axis=1)
    out_terms = jnp.einsum("tsk,skn->stn", h_sel, w_dn, preferred_element_type=jnp.float32)
    out_part = (
        place_terms(out_terms, live_dn, d_of_dn, d_blocks)
        .transpose(1, 0, 2)
        .reshape(tok_rows, full_width)
    )
    output = lax.psum_scatter(out_part, "row", scatter_dimension=1, tiled=True).astype(jnp.bfloat16)
    grad_all = lax.all_gather(grad_out, "row", axis=1, tiled=True)
    g_sel = jnp.take(grad_all.reshape(tok_rows, d_blocks, block_size), d_of_dn, axis=1)
    back_terms = jnp.einsum("tsn,skn->stk", g_sel, w_dn, preferred_element_type=jnp.float32)
    grad_hidden = (
        place_terms(back_terms, live_dn, f_of_dn, panel_cols)
        .transpose(1, 0, 2)
        .reshape(tok_rows, panel_cols * block_size)
    )
    grad_gate = (grad_hidden * gate_up[1] * slope_term).astype(jnp.bfloat16)
    grad_up = (grad_hidden * act_f).astype(jnp.bfloat16)
    grad_pair = jnp.stack([grad_gate, grad_up]).reshape(2, tok_rows, panel_cols, block_size)
    gu_sel = jnp.take(grad_pair, f_of_gu, axis=2)
    in_terms = jnp.einsum("gtsn,gskn->stk", gu_sel, w_gu, preferred_element_type=jnp.float32)
    in_part = (
        place_terms(in_terms, live_gu, d_of_gu, d_blocks)
        .transpose(1, 0, 2)
        .reshape(tok_rows, full_width)
    )
    grad_in = lax.psum_scatter(in_part, "row", scatter_dimension=1, tiled=True).astype(jnp.bfloat16)
    x_every, g_every = (
        lax.all_to_all(gathered, "col", split_axis=1, concat_axis=0, tiled=True),
        lax.all_to_all(grad_all, "col", split_axis=1, concat_axis=0, tiled=True),
    )
    h_every, pair_every = (
        lax.all_gather(hidden, "col", axis=0, tiled=True),
        lax.all_gather(grad_pair, "col", axis=1, tiled=True),
    )
    all_rows = x_every.shape[0]
    own_live_gu = (slot_range < gate_up_count[0, 0]).astype(jnp.float32)
    own_live_dn = (slot_range < down_count[0, 0]).astype(jnp.float32)
    own_d_gu = gate_up_index[0] // panel_cols
    own_f_gu = gate_up_index[0] % panel_cols
    own_f_dn = down_index[0] // half_rows
    own_d_dn = down_index[0] % half_rows
    xs_own = jnp.take(x_every.reshape(all_rows, half_rows, block_size), own_d_gu, axis=1)
    gs_own = jnp.take(pair_every, own_f_gu, axis=2)
    dw_gu = (
        jnp.einsum("tsk,gtsn->gskn", xs_own, gs_own, preferred_element_type=jnp.float32)
        * own_live_gu[None, :, None, None]
    )
    hs_own = jnp.take(h_every.reshape(all_rows, panel_cols, block_size), own_f_dn, axis=1)
    ys_own = jnp.take(g_every.reshape(all_rows, half_rows, block_size), own_d_dn, axis=1)
    dw_dn = (
        jnp.einsum("tsk,tsn->skn", hs_own, ys_own, preferred_element_type=jnp.float32)
        * own_live_dn[:, None, None]
    )
    grad_gate_up = dw_gu.reshape(2, 1, slot_count, block_size, block_size)
    grad_down = dw_dn.reshape(1, slot_count, block_size, block_size)
    return (output, grad_in, grad_gate_up, grad_down)


def solution(mesh):
    placed = (
        P(("groups", "col"), "row"),
        P(None, "col", "row", None, None),
        P("col", "row"),
        P("col", "row"),
        P("col", "row", None, None),
        P("col", "row"),
        P("col", "row"),
        P(("groups", "col"), "row"),
    )
    return jax.shard_map(
        per_device,
        mesh=mesh,
        in_specs=placed,
        out_specs=(
            P(("groups", "col"), "row"),
            P(("groups", "col"), "row"),
            P(None, ("groups", "col"), "row", None, None),
            P(("groups", "col"), "row", None, None),
        ),
        check_vma=False,
    )
```

profile of v0, /device:TPU:0, one launch (start us, length us, event | category | flops | bytes accessed | tf_op | source)
XLA Modules:
  0.0 1105.4 jit_solution(5727976883491939800)
XLA Ops:
  13.3 1.9 all-reduce.2
  15.3 1.8 all-gather.1
  18.3 1.8 all-gather
  20.8 52.7 %all-gather.9.cloned.1.call-done = bf16[192,8192]{1,0:T(8,128)(2,1)} async-done(((bf16[192,1024]{1,0:T(8,128)(2,1)}), bf16[192,8192]{1,0:T(8,128)(2,1)}) %all-gather.9.cloned.1.call-update) | async-done | bytes 3145744 | tf_op jit(solution)/shard_map/all_gather | solution.py:35
  73.5 2.8 copy_bitcast_fusion.5
  76.2 16.6 %gather_fusion.4 = bf16[512,192,128]{2,1,0:T(8,128)(2,1)} fusion(bf16[192,64,128]{2,0,1:T(8,128)(2,1)S(1)} %copy_bitcast_fusion.5, s32[1024]{0:T(1024)S(1)} %pad_clamp_fusion.7), kind=kCustom, calls=%fused_computation.clone | custom fusion | bytes 50333696 | tf_op jit(solution)/shard_map/jit(_take)/gather | solution.py:45
  92.9 41.9 %all-gather.15.cloned.1.call-done = bf16[192,8192]{1,0:T(8,128)(2,1)} async-done(((bf16[192,1024]{1,0:T(8,128)(2,1)}), bf16[192,8192]{1,0:T(8,128)(2,1)}) %all-gather.15.cloned.1.call-update) | async-done | bytes 3145744 | tf_op jit(solution)/shard_map/all_gather | solution.py:70
  134.8 2.8 copy_bitcast_fusion.4
  137.6 20.2 %gather_fusion.5 = bf16[512,192,128]{2,1,0:T(8,128)(2,1)} fusion(bf16[192,64,128]{2,0,1:T(8,128)(2,1)S(1)} %copy_bitcast_fusion.4, s32[1024]{0:T(1024)S(1)} %pad_clamp_fusion.5), kind=kCustom, calls=%fused_computation.2.clone | custom fusion | bytes 50333696 | tf_op jit(solution)/shard_map/jit(_take)/gather | solution.py:71
  157.8 7.3 all-gather.13.cloned.1.call-done
  165.1 40.1 %broadcast_multiply_fusion = f32[512,192,128]{2,1,0:T(8,128)} fusion(f32[512]{0:T(512)S(1)} %bitcast.280, bf16[512,128,128]{2,1,0:T(8,128)(2,1)} %bitcast.267, bf16[512,192,128]{2,1,0:T(8,128)(2,1)} %gather_fusion.5, pred[512]{0:T(512)(128)(4,1)S(1)} %compare_and_fusion.2), kind=kOutput, calls=%fused_computation.40 | convolution fusion | flops 3246391296 | bytes 92277248 | tf_op jit(solution)/shard_map/tsn,skn->stk/dot_general | solution.py:72
  205.4 80.7 %scatter_fusion.2 = f32[16,192,128]{2,1,0:T(8,128)S(1)} fusion(f32[16,192,128]{2,1,0:T(8,128)S(1)} %broadcast_in_dim.73, s32[512]{0:T(512)S(1)} %bitcast.290, f32[512,192,128]{2,1,0:T(8,128)} %broadcast_multiply_fusion), kind=kCustom, calls=%fused_computation.10 | custom fusion | flops 12582912 | bytes 150996992 | tf_op jit(solution)/shard_map/scatter-add | solution.py:11
  286.2 23.6 %copy.42 = bf16[2,2,256,128,128]{4,3,0,2,1:T(8,128)(2,1)} copy(bf16[2,2,256,128,128]{4,3,2,1,0:T(8,128)(2,1)} %all-gather.11.cloned.1.call-done) | data formatting | bytes 67108864 | tf_op jit(solution)/shard_map/all_gather | solution.py:37
  309.8 54.4 %multiply_bitcast_fusion = f32[512,2,192,128]{3,2,1,0:T(8,128)} fusion(f32[512]{0:T(512)S(1)} %bitcast.282, bf16[2,512,128,128]{3,2,0,1:T(8,128)(2,1)} %bitcast.265, bf16[512,192,128]{2,1,0:T(8,128)(2,1)} %gather_fusion.4, pred[512]{0:T(512)(128)(4,1)S(1)} %compare_and_fusion.3), kind=kOutput, calls=%fused_computation.12 | convolution fusion | flops 6480199680 | bytes 159386112 | tf_op jit(solution)/shard_map/tsk,gskn->sgtn/dot_general | solution.py:46
  364.6 151.6 %scatter_fusion = f32[16,2,192,128]{3,2,1,0:T(8,128)S(1)} fusion(f32[16,2,192,128]{3,2,1,0:T(8,128)S(1)} %broadcast_in_dim.70, s32[512]{0:T(512)S(1)} %bitcast.294, f32[512,2,192,128]{3,2,1,0:T(8,128)} %multiply_bitcast_fusion), kind=kCustom, calls=%fused_computation.8 | custom fusion | flops 25165824 | bytes 301991936 | tf_op jit(solution)/shard_map/scatter-add | solution.py:11
  516.3 3.5 fusion.55
  519.7 0.9 copy.49
  520.7 0.9 copy.50
  521.6 2.0 fusion.50
  523.7 2.7 pad_maximum_fusion
  526.4 22.1 %gather_fusion.1 = bf16[512,2,192,128]{3,2,1,0:T(8,128)(2,1)} fusion(bf16[2,192,16,128]{3,1,0,2:T(8,128)(2,1)} %pad_maximum_fusion, s32[1024]{0:T(1024)S(1)} %pad_clamp_fusion.4), kind=kCustom, calls=%fused_computation.5 | custom fusion | bytes 100665344 | tf_op jit(solution)/shard_map/jit(_take)/gather | solution.py:81
  548.6 46.6 %bitcast_multiply_fusion = f32[512,192,128]{2,1,0:T(8,128)} fusion(f32[512]{0:T(512)S(1)} %bitcast.283, bf16[2,512,128,128]{3,2,0,1:T(8,128)(2,1)} %bitcast.266, bf16[512,2,192,128]{3,2,1,0:T(8,128)(2,1)} %gather_fusion.1, pred[512]{0:T(512)(128)(4,1)S(1)} %compare_and_fusion.6), kind=kOutput, calls=%fused_computation.15 | convolution fusion | flops 6480199680 | bytes 134220288 | tf_op jit(solution)/shard_map/gtsn,gskn->stk/dot_general | solution.py:82
  595.2 3.5 broadcast.289.clone.1
  598.7 124.2 %scatter_fusion.3 = f32[64,192,128]{2,1,0:T(8,128)} fusion(f32[64,192,128]{2,1,0:T(8,128)} %broadcast.289.clone.1, s32[512]{0:T(512)S(1)} %bitcast.289, f32[512,192,128]{2,1,0:T(8,128)} %bitcast_multiply_fusion), kind=kCustom, calls=%fused_computation.11 | custom fusion | flops 12582912 | bytes 150996992 | tf_op jit(solution)/shard_map/scatter-add | solution.py:11
  722.9 6.2 copy_bitcast_fusion
  729.3 1.3 fusion.57
  730.6 18.0 %gather_fusion = bf16[512,192,128]{2,1,0:T(8,128)(2,1)} fusion(bf16[192,16,128]{2,0,1:T(8,128)(2,1)} %fusion.57, s32[1024]{0:T(1024)S(1)} %pad_clamp_fusion.6), kind=kCustom, calls=%fused_computation.4 | custom fusion | bytes 50333696 | tf_op jit(solution)/shard_map/jit(_take)/gather | solution.py:62
  748.5 34.3 %broadcast_multiply_fusion.1 = f32[512,192,128]{2,1,0:T(8,128)} fusion(f32[512]{0:T(512)S(1)} %bitcast.281, bf16[512,128,128]{2,1,0:T(8,128)(2,1)} %bitcast.268, bf16[512,192,128]{2,1,0:T(8,128)(2,1)} %gather_fusion, pred[512]{0:T(512)(128)(4,1)S(1)} %compare_and_fusion.7), kind=kOutput, calls=%fused_computation.41 | convolution fusion | flops 3246391296 | bytes 92277248 | tf_op jit(solution)/shard_map/tsk,skn->stn/dot_general | solution.py:63
  782.8 3.5 broadcast.289.clone
  786.3 125.6 %scatter_fusion.1 = f32[64,192,128]{2,1,0:T(8,128)} fusion(f32[64,192,128]{2,1,0:T(8,128)} %broadcast.289.clone, s32[512]{0:T(512)S(1)} %bitcast.286, f32[512,192,128]{2,1,0:T(8,128)} %broadcast_multiply_fusion.1), kind=kCustom, calls=%fused_computation.9 | custom fusion | flops 12582912 | bytes 150996992 | tf_op jit(solution)/shard_map/scatter-add | solution.py:11
  911.8 6.3 copy_bitcast_fusion.1
  918.5 6.4 all_to_all.32
  924.9 0.8 copy.78
  925.8 1.2 copy.47
  927.4 6.5 all_to_all.33
  933.8 0.8 copy.81
  934.7 2.9 copy.54
  937.6 12.7 %gather_fusion.6 = bf16[256,384,128]{2,1,0:T(8,128)(2,1)} fusion(bf16[384,32,128]{2,0,1:T(8,128)(2,1)S(1)} %copy.47, s32[1024]{0:T(1024)S(1)} %pad_clamp_fusion.2), kind=kCustom, calls=%fused_computation.1.clone | custom fusion | bytes 50332672 | tf_op jit(solution)/shard_map/jit(_take)/gather | solution.py:104
  950.2 14.4 %gather_fusion.7 = bf16[256,384,128]{2,1,0:T(8,128)(2,1)} fusion(bf16[384,32,128]{2,0,1:T(8,128)(2,1)} %copy.54, s32[1024]{0:T(1024)S(1)} %pad_clamp_fusion), kind=kCustom, calls=%fused_computation.3.clone | custom fusion | bytes 50332672 | tf_op jit(solution)/shard_map/jit(_take)/gather | solution.py:111
  964.7 1.9 copy.51
  966.5 1.0 copy.52
  967.5 12.5 %gather_fusion.3 = bf16[256,384,128]{2,1,0:T(8,128)(2,1)} fusion(bf16[384,16,128]{2,0,1:T(8,128)(2,1)S(1)} %copy.52, s32[1024]{0:T(1024)S(1)} %pad_clamp_fusion.1), kind=kCustom, calls=%fused_computation.7 | custom fusion | bytes 50332672 | tf_op jit(solution)/shard_map/jit(_take)/gather | solution.py:110
  980.0 24.0 %multiply_bitcast_fusion.2 = f32[1,256,128,128]{3,2,1,0:T(8,128)} fusion(bf16[256,384,128]{2,1,0:T(8,128)(2,1)} %gather_fusion.7, pred[256]{0:T(512)(128)(4,1)S(1)} %get-tuple-element.24, bf16[256,384,128]{2,1,0:T(8,128)(2,1)} %gather_fusion.3, pred[256]{0:T(512)(128)(4,1)S(1)} %get-tuple-element.37, f32[256]{0:T(256)S(1)} %compare_convert_fusion.2), kind=kOutput, calls=%fused_computation.48 | convolution fusion | flops 3250585600 | bytes 67110400 | tf_op jit(solution)/shard_map/tsk,tsn->skn/dot_general | solution.py:113
  1004.0 21.2 %gather_fusion.2 = bf16[256,2,384,128]{3,2,1,0:T(8,128)(2,1)} fusion(bf16[2,384,16,128]{3,1,0,2:T(8,128)(2,1)} %all-gather.17.cloned.1.call-done, s32[1024]{0:T(1024)S(1)} %pad_clamp_fusion.3), kind=kCustom, calls=%fused_computation.6 | custom fusion | bytes 100664320 | tf_op jit(solution)/shard_map/jit(_take)/gather | solution.py:105
  1025.2 37.9 %multiply_bitcast_fusion.1 = f32[2,1,256,128,128]{3,4,0,2,1:T(8,128)} fusion(f32[256]{0:T(256)S(1)} %compare_convert_fusion.3, bf16[256,384,128]{2,1,0:T(8,128)(2,1)} %gather_fusion.6, pred[256]{0:T(512)(128)(4,1)S(1)} %get-tuple-element.26, bf16[256,2,384,128]{3,2,1,0:T(8,128)(2,1)} %gather_fusion.2, pred[256]{0:T(512)(128)(4,1)S(1)} %get-tuple-element.38), kind=kOutput, calls=%fused_computation.22 | convolution fusion | flops 6488588288 | bytes 109053440 | tf_op jit(solution)/shard_map/tsk,gtsn->gskn/dot_general | solution.py:107
  1063.2 31.1 %copy.56 = f32[2,1,256,128,128]{4,3,2,1,0:T(8,128)} copy(f32[2,1,256,128,128]{3,4,0,2,1:T(8,128)} %multiply_bitcast_fusion.1) | data formatting | bytes 67108864
  1094.3 1.9 convert_element_type.68
  1096.2 1.9 convert_element_type.65
  (104 shorter events, 8.0 us)
Async XLA Ops:
  7.2 4.2 copy-start.19
  7.2 8.2 copy-start.14
  7.2 11.1 %copy-start.16 = (s32[1,256]{1,0:T(1,128)S(1)}, s32[1,256]{1,0:T(1,128)}, u32[]{:S(2)}) copy-start(s32[1,256]{1,0:T(1,128)} %param.17) | copy-start | bytes 3076
  7.2 66.3 %all-gather.9.cloned.1.call-start = ((), (), s32[]{:S(2)}) async-start(), calls=%async_computation.4 | async-start | bytes 3538944 | tf_op jit(solution)/shard_map/all_gather | solution.py:35
  7.9 126.9 %all-gather.15.cloned.1.call-start = ((), (), s32[]{:S(2)}) async-start(), calls=%async_computation.8 | async-start | bytes 3538944 | tf_op jit(solution)/shard_map/all_gather | solution.py:70
  8.7 156.4 %all-gather.13.cloned.1.call-start = ((), (), s32[]{:S(2)}) async-start(), calls=%async_computation.6 | async-start | bytes 25165824 | tf_op jit(solution)/shard_map/all_gather | solution.py:54
  9.4 276.8 %all-gather.11.cloned.1.call-start = ((), (), s32[]{:S(2)}) async-start(), calls=%async_computation.5 | async-start | bytes 50331648 | tf_op jit(solution)/shard_map/all_gather | solution.py:37
  10.0 954.7 %all-gather.19.cloned.1.call-start = ((), (), s32[]{:S(2)}) async-start(), calls=%async_computation.11 | async-start | bytes 2359296 | tf_op jit(solution)/shard_map/all_gather | solution.py:94
  17.7 3.0 copy-start.7
  18.3 146.8 %copy-start.3 = (f32[1,2,2,128]{3,1,2,0:T(2,128)}, f32[1,2,2,128]{3,1,2,0:T(2,128)S(1)}, u32[]{:S(2)}) copy-start(f32[1,2,2,128]{3,1,2,0:T(2,128)S(1)} %copy.76) | copy-start | bytes 6148
  20.1 0.6 copy-start.11
  20.1 0.6 copy-start.5
  20.1 185.3 %copy-start.9 = (s32[1,2,2,128]{3,1,2,0:T(2,128)}, s32[1,2,2,128]{3,1,2,0:T(2,128)S(1)}, u32[]{:S(2)}) copy-start(s32[1,2,2,128]{3,1,2,0:T(2,128)S(1)} %copy.71) | copy-start | bytes 6148
  286.1 23.7 %copy-start = (f32[16,192,128]{2,1,0:T(8,128)}, f32[16,192,128]{2,1,0:T(8,128)S(1)}, u32[]{:S(2)}) copy-start(f32[16,192,128]{2,1,0:T(8,128)S(1)} %scatter_fusion.2) | copy-start | bytes 4718596
  309.8 54.8 %copy-start.13 = (s32[1,2,2,128]{3,1,2,0:T(2,128)S(1)}, s32[1,2,2,128]{3,1,2,0:T(2,128)}, u32[]{:S(2)}) copy-start(s32[1,2,2,128]{3,1,2,0:T(2,128)} %copy.72) | copy-start | bytes 6148
  516.2 7.4 copy-start.18
  523.6 480.4 %all-gather.17.cloned.1.call-start = ((), (), s32[]{:S(2)}) async-start(), calls=%async_computation.10 | async-start | bytes 4718592 | tf_op jit(solution)/shard_map/all_gather | solution.py:95
  548.5 50.2 %copy-start.8 = (s32[1,2,2,128]{3,1,2,0:T(2,128)S(1)}, s32[1,2,2,128]{3,1,2,0:T(2,128)}, u32[]{:S(2)}) copy-start(s32[1,2,2,128]{3,1,2,0:T(2,128)} %copy-done.7) | copy-start | bytes 6148
  548.5 545.8 %reduce-scatter.5.cloned.1.call-start = ((), (), s32[]{:S(2)}) async-start(), calls=%async_computation.9 | async-start | bytes 7077888 | tf_op jit(solution)/shard_map/reduce_scatter | solution.py:88
  722.9 6.2 copy-start.12
  722.9 6.3 copy-start.10
  729.1 367.1 %reduce-scatter.3.cloned.1.call-start = ((), (), s32[]{:S(2)}) async-start(), calls=%async_computation.7 | async-start | bytes 7077888 | tf_op jit(solution)/shard_map/reduce_scatter | solution.py:69
  730.6 18.0 %copy-start.4 = (f32[1,2,2,128]{3,1,2,0:T(2,128)S(1)}, f32[1,2,2,128]{3,1,2,0:T(2,128)}, u32[]{:S(2)}) copy-start(f32[1,2,2,128]{3,1,2,0:T(2,128)} %copy-done.3) | copy-start | bytes 6148
  748.5 37.7 %copy-start.6 = (s32[1,2,2,128]{3,1,2,0:T(2,128)S(1)}, s32[1,2,2,128]{3,1,2,0:T(2,128)}, u32[]{:S(2)}) copy-start(s32[1,2,2,128]{3,1,2,0:T(2,128)} %copy-done.5) | copy-start | bytes 6148
  911.8 6.3 copy-start.15
  911.8 6.4 copy-start.17
  911.8 6.5 copy-start.1
  918.1 8.9 copy-start.2
Sparse Core Ops, SparseCore 0:
  10.2 63.1 all-gather.8
  75.6 59.1 all-gather.14
  136.4 28.6 all-gather.12
  166.5 52.3 all-gather.10
  523.7 11.1 all-gather.18
  548.6 13.3 all-gather.16
  729.3 119.3 reduce-scatter.4
  918.3 119.3 reduce-scatter.2
where the time goes:
time: 1120 us; the launch traced here: 1110 us
  other arithmetic  496 us (44%)
  matrix products  237 us (21%)
  local copies, waits for them, and re-layouts  232 us (21%)
  waiting for transfers between devices  105 us (9%)
  blocking collectives  18.4 us (2%)
  between operations  16.4 us (1%)
    scatter-add x4, other arithmetic, place_terms(): return jax.ops.segment_sum(masked, targets, num_segments=count)  482 us
    dot_general x1, matrix products, per_device(): jnp.einsum('tsk,gskn->sgtn', x_sel, w_gu, preferred_element_type=jnp.floa...  54.4 us
    all_gather x1, waiting for transfers between devices, per_device(): gathered = lax.all_gather(tokens, 'row', axis=1, tiled=True)  52.7 us
    dot_general x1, matrix products, per_device(): jnp.einsum('gtsn,gskn->stk', gu_sel, w_gu, preferred_element_type=jnp.flo...  46.6 us
    all_gather x1, waiting for transfers between devices, per_device(): grad_all = lax.all_gather(grad_out, 'row', axis=1, tiled=True)  41.9 us
    dot_general x1, matrix products, per_device(): jnp.einsum('tsn,skn->stk', g_sel, w_dn, preferred_element_type=jnp.float32)  40.1 us
    dot_general x1, matrix products, per_device(): jnp.einsum('tsk,gtsn->gskn', xs_own, gs_own, preferred_element_type=jnp.f...  37.9 us
    unnamed x56, local copies, waits for them, and re-layouts  35.9 us
  transfers between devices with their start and end apart: 8, of which 3 were waited for; matrix products, arithmetic and copies ran while one was open for 66% of the time, Pallas kernels for 0%

commit v1 on v0

v1 whole, which is shorter than its diff:
```python
import functools

import jax
import jax.numpy as jnp
from jax import lax
from jax.experimental import pallas as pl
from jax.experimental.pallas import tpu as pltpu
from jax.sharding import PartitionSpec as P

FFW = 16384
F32 = jnp.float32
BF16 = jnp.bfloat16


def clear(ref):
    def body(i, carry):
        ref[i] = jnp.zeros(ref.shape[1:], ref.dtype)
        return carry

    lax.fori_loop(0, ref.shape[0], body, 0)


def live_slots(count, chunk):
    base = pl.program_id(0) * chunk
    return base, jnp.clip(count[0] - base, 0, chunk)


def dot_nt(a, b):
    return lax.dot_general(a, b, (((1,), (1,)), ((), ())), preferred_element_type=F32)


def gate_up_kernel(cols, chunk, index, count, x, w, acc):
    @pl.when(pl.program_id(0) == 0)
    def _():
        clear(acc)

    base, live = live_slots(count, chunk)

    def body(i, carry):
        p = index[base + i]
        pair = jnp.concatenate([w[0, i], w[1, i]], axis=1)
        acc[lax.rem(p, cols)] += jnp.dot(x[lax.div(p, cols)], pair, preferred_element_type=F32)
        return carry

    lax.fori_loop(0, live, body, 0)


def down_kernel(rows, chunk, index, count, h, g, w, out, back):
    @pl.when(pl.program_id(0) == 0)
    def _():
        clear(out)
        clear(back)

    base, live = live_slots(count, chunk)

    def body(i, carry):
        p = index[base + i]
        f, d = lax.div(p, rows), lax.rem(p, rows)
        out[d] += jnp.dot(h[f], w[i], preferred_element_type=F32)
        back[f] += dot_nt(g[d], w[i])
        return carry

    lax.fori_loop(0, live, body, 0)


def grad_in_kernel(cols, chunk, index, count, grads, w, out):
    @pl.when(pl.program_id(0) == 0)
    def _():
        clear(out)

    base, live = live_slots(count, chunk)

    def body(i, carry):
        p = index[base + i]
        pair = jnp.concatenate([w[0, i], w[1, i]], axis=1)
        out[lax.div(p, cols)] += dot_nt(grads[lax.rem(p, cols)], pair)
        return carry

    lax.fori_loop(0, live, body, 0)


def grad_gate_up_kernel(cols, chunk, index, count, xt, grads, dw):
    base, live = live_slots(count, chunk)
    size = dw.shape[-1]

    def body(i, carry):
        p = index[base + i]
        both = jnp.dot(xt[lax.div(p, cols)], grads[lax.rem(p, cols)], preferred_element_type=F32)
        dw[0, i] = both[:, :size]
        dw[1, i] = both[:, size:]
        return carry

    def empty(i, carry):
        dw[0, i] = jnp.zeros((size, size), F32)
        dw[1, i] = jnp.zeros((size, size), F32)
        return carry

    lax.fori_loop(0, live, body, 0)
    lax.fori_loop(live, chunk, empty, 0)


def grad_down_kernel(rows, chunk, index, count, ht, g, dw):
    base, live = live_slots(count, chunk)
    size = dw.shape[-1]

    def body(i, carry):
        p = index[base + i]
        dw[i] = jnp.dot(ht[lax.div(p, rows)], g[lax.rem(p, rows)], preferred_element_type=F32)
        return carry

    def empty(i, carry):
        dw[i] = jnp.zeros((size, size), F32)
        return carry

    lax.fori_loop(0, live, body, 0)
    lax.fori_loop(live, chunk, empty, 0)


def whole(shape):
    return pl.BlockSpec(shape, lambda *_: (0,) * len(shape))


def pair_chunk(chunk, size):
    return pl.BlockSpec((2, chunk, size, size), lambda s, *_: (0, s, 0, 0))


def one_chunk(chunk, size):
    return pl.BlockSpec((chunk, size, size), lambda s, *_: (s, 0, 0))


def run(kernel, steps, flops, index, count, operands, in_specs, out_shape, out_specs):
    return pl.pallas_call(
        kernel,
        out_shape=out_shape,
        grid_spec=pltpu.PrefetchScalarGridSpec(
            num_scalar_prefetch=2,
            grid=(steps,),
            in_specs=in_specs,
            out_specs=out_specs,
        ),
        compiler_params=pltpu.CompilerParams(
            dimension_semantics=("arbitrary",), vmem_limit_bytes=50 * 1024 * 1024
        ),
        cost_estimate=pl.CostEstimate(flops=flops, bytes_accessed=32 << 20, transcendentals=0),
    )(index, count, *operands)


def per_device(
    tokens,
    gate_up_blocks,
    gate_up_index,
    gate_up_count,
    down_blocks,
    down_index,
    down_count,
    grad_out,
):
    n_row = lax.axis_size("row")
    n_col = lax.axis_size("col")
    col = lax.axis_index("col")
    size = gate_up_blocks.shape[-1]
    slots = gate_up_blocks.shape[2]
    width = tokens.shape[1] * n_row
    half = width // n_col
    rows = half // size
    cols = FFW // (n_row * size)
    t = tokens.shape[0]
    both = 2 * t
    chunk = min(32, slots)
    steps = slots // chunk
    unit = 4 * slots * both * size * size
    swap = [(0, 1), (1, 0)]

    def exchange(a):
        return lax.ppermute(a, "col", swap)

    def spread(a):
        all_width = lax.all_gather(a, "row", axis=1, tiled=True)
        own = lax.dynamic_slice_in_dim(all_width, col * half, half, 1)
        other = exchange(lax.dynamic_slice_in_dim(all_width, (1 - col) * half, half, 1))
        return jnp.concatenate([own, other], axis=0).reshape(both, rows, size)

    x_flat = spread(tokens)
    g_flat = spread(grad_out)
    x = x_flat.transpose(1, 0, 2)
    xt = x_flat.transpose(1, 2, 0)
    g = g_flat.transpose(1, 0, 2)
    w_gu = gate_up_blocks[:, 0]
    w_dn = down_blocks[0]
    gu_index, gu_count = gate_up_index[0], gate_up_count[0]
    dn_index, dn_count = down_index[0], down_count[0]

    def shape(*dims):
        return jax.ShapeDtypeStruct(dims, F32)

    part = run(
        functools.partial(gate_up_kernel, cols, chunk), steps, unit, gu_index, gu_count, (x, w_gu),
        [whole((rows, both, size)), pair_chunk(chunk, size)],
        shape(cols, both, 2 * size), whole((cols, both, 2 * size)),
    )
    gate_up = part[:, :t] + exchange(part[:, t:])
    gate, up = gate_up[..., :size], gate_up[..., size:]
    sigmoid = jax.nn.sigmoid(gate)
    act = gate * sigmoid
    slope = sigmoid * (1.0 + gate * (1.0 - sigmoid))
    hidden = (act * up).astype(BF16)
    h = jnp.concatenate([hidden, exchange(hidden)], axis=1)
    out_part, back_part = run(
        functools.partial(down_kernel, rows, chunk), steps, unit, dn_index, dn_count, (h, g, w_dn),
        [whole((cols, both, size)), whole((rows, both, size)), one_chunk(chunk, size)],
        (shape(rows, both, size), shape(cols, both, size)),
        (whole((rows, both, size)), whole((cols, both, size))),
    )

    def collect(a):
        own, other = a[:, :t], exchange(a[:, t:])
        full = jnp.where(
            col == 0,
            jnp.concatenate([own, other], axis=0),
            jnp.concatenate([other, own], axis=0),
        )
        mine = lax.psum_scatter(full, "row", scatter_dimension=0, tiled=True)
        return mine.transpose(1, 0, 2).reshape(t, width // n_row).astype(BF16)

    output = collect(out_part)
    grad_hidden = back_part[:, :t] + exchange(back_part[:, t:])
    grads_own = jnp.concatenate(
        [(grad_hidden * up * slope).astype(BF16), (grad_hidden * act).astype(BF16)], axis=-1
    )
    grads = jnp.concatenate([grads_own, exchange(grads_own)], axis=1)
    in_part = run(
        functools.partial(grad_in_kernel, cols, chunk), steps, unit, gu_index, gu_count, (grads, w_gu),
        [whole((cols, both, 2 * size)), pair_chunk(chunk, size)],
        shape(rows, both, size), whole((rows, both, size)),
    )
    grad_in = collect(in_part)
    dw_gu = run(
        functools.partial(grad_gate_up_kernel, cols, chunk), steps, unit, gu_index, gu_count, (xt, grads),
        [whole((rows, size, both)), whole((cols, both, 2 * size))],
        shape(2, slots, size, size), pair_chunk(chunk, size),
    )
    dw_dn = run(
        functools.partial(grad_down_kernel, rows, chunk), steps, unit // 2, dn_index, dn_count,
        (h.transpose(0, 2, 1), g),
        [whole((cols, size, both)), whole((rows, both, size))],
        shape(slots, size, size), one_chunk(chunk, size),
    )
    return (output, grad_in, dw_gu[:, None], dw_dn[None])


def solution(mesh):
    placed = (
        P(("groups", "col"), "row"),
        P(None, "col", "row", None, None),
        P("col", "row"),
        P("col", "row"),
        P("col", "row", None, None),
        P("col", "row"),
        P("col", "row"),
        P(("groups", "col"), "row"),
    )
    return jax.shard_map(
        per_device,
        mesh=mesh,
        in_specs=placed,
        out_specs=(
            P(("groups", "col"), "row"),
            P(("groups", "col"), "row"),
            P(None, ("groups", "col"), "row", None, None),
            P(("groups", "col"), "row", None, None),
        ),
        check_vma=False,
    )
```

time: 1120 us -> 527 us (0.47); the launches traced: 1110 us -> 528 us
  other arithmetic: 496 us -> 43.8 us
  matrix products: 237 us -> 0 us
  Pallas kernels: 0 us -> 191 us
  local copies, waits for them, and re-layouts: 232 us -> 90.1 us
  waiting for transfers between devices: 105 us -> 185 us
  blocking collectives: 18.4 us -> 0 us
    scatter-add x4 -> x0, other arithmetic: 482 us -> none  [place_terms(): return jax.ops.segment_sum(masked, targets, num_segments=count)]
    dot_general x6 -> x0, matrix products: 237 us -> none  [the longest x1 54.4 us: per_device(): jnp.einsum('tsk,gskn->sgtn', x_sel, w_gu, preferred_element_type=jnp.floa...]
    pallas_call x0 -> x5, Pallas kernels: none -> 191 us  [run(): pl.pallas_call(kernel, out_shape=out_shape, grid_spec=pltpu.PrefetchScala...]
    gather x8 -> x0, local copies, waits for them, and re-layouts: 138 us -> none  [the longest x1 22.1 us: per_device(): gu_sel = jnp.take(grad_pair, f_of_gu, axis=2)]
    reduce_scatter x2, waiting for transfers between devices: 0.01 us -> 98.7 us  [collect(): mine = lax.psum_scatter(full, 'row', scatter_dimension=0, tiled=True)]
    all_gather x6 -> x2, waiting for transfers between devices: 102 us -> 68 us  [spread(): all_width = lax.all_gather(a, 'row', axis=1, tiled=True)]
    all_gather x2 -> x0, local copies, waits for them, and re-layouts: 25.5 us -> none  [the longest x1 23.6 us: per_device(): lax.all_gather(gate_up_blocks, 'col', axis=1, tiled=True)]
    unnamed x56 -> x18, local copies, waits for them, and re-layouts: 35.9 us -> 15.4 us
  transfers between devices with their start and end apart: 8 -> 12, of which waited for: 3 -> 7; matrix products, arithmetic and copies ran while one was open for 66% -> 19% of each run, Pallas kernels for 0% -> 31%
where the time goes in v1:
time: 527 us; the launch traced here: 528 us
  Pallas kernels  191 us (36%)
  waiting for transfers between devices  185 us (35%)
  local copies, waits for them, and re-layouts  90.1 us (17%)
  other arithmetic  43.8 us (8%)
  between operations  15.2 us (3%)
    pallas_call x5, Pallas kernels, run(): pl.pallas_call(kernel, out_shape=out_shape, grid_spec=pltpu.PrefetchScala...  191 us
    reduce_scatter x2, waiting for transfers between devices, collect(): mine = lax.psum_scatter(full, 'row', scatter_dimension=0, tiled=True)  98.7 us
    all_gather x2, waiting for transfers between devices, spread(): all_width = lax.all_gather(a, 'row', axis=1, tiled=True)  68 us
    ppermute x8, waiting for transfers between devices, exchange(): return lax.ppermute(a, 'col', swap)  17.6 us
    ppermute x5, local copies, waits for them, and re-layouts, exchange(): return lax.ppermute(a, 'col', swap)  17.5 us
    unnamed x18, local copies, waits for them, and re-layouts  15.4 us
    select_n x2, other arithmetic, collect(): jnp.where(col == 0, jnp.concatenate([own, other], axis=0), jnp.concatenat...  10.8 us
  transfers between devices with their start and end apart: 12, of which 7 were waited for; matrix products, arithmetic and copies ran while one was open for 19% of the time, Pallas kernels for 31%

profile of v1, /device:TPU:0, one launch (start us, length us, event | category | flops | bytes accessed | tf_op | source)
XLA Modules:
  0.0 527.9 jit_solution(15059941470510536715)
XLA Ops:
  7.9 2.0 copy.42
  10.0 63.4 %all-gather.3.cloned.1.call-done = bf16[192,8192]{1,0:T(8,128)(2,1)} async-done(((bf16[192,1024]{1,0:T(8,128)(2,1)}), bf16[192,8192]{1,0:T(8,128)(2,1)}) %all-gather.3.cloned.1.call-update) | async-done | bytes 3145744 | tf_op jit(solution)/shard_map/all_gather | solution.py:178
  73.4 2.1 constant_dynamic-slice_fusion.3
  76.3 2.7 collective-permute-done
  79.1 2.0 pad_maximum_fusion
  81.1 3.6 copy.36
  84.7 2.9 copy.37.x
  87.5 1.9 copy-done.1
  89.4 47.4 %shard_map.111 = f32[16,384,256]{2,1,0:T(8,128)} custom-call(s32[256]{0:T(256)S(1)} %bitcast.38, s32[1]{0:T(128)} %bitcast.31.count, bf16[32,384,128]{2,1,0:T(8,128)(2,1)S(1)} %copy-done.1, bf16[2,256,128,128]{3,2,1,0:T(8,128)(2,1)} %bitcast.43), custom_call_target="tpu_custom_call" | custom-call | flops 6442450944 | bytes 33554432 | tf_op jit(solution)/shard_map/pallas_call | solution.py:132
  136.8 6.2 %fusion.3 = (f32[16,192,256]{2,1,0:T(8,128)}, f32[16,192,256]{2,1,0:T(8,128)}) fusion(f32[16,384,256]{2,1,0:T(8,128)} %shard_map.111), kind=kLoop, calls=%fused_computation.23 | loop fusion | bytes 12582912 | tf_op jit(solution)/shard_map/slice | solution.py:201
  143.0 4.6 all-gather.5.cloned.1.call-done
  147.7 4.5 constant_dynamic-slice_fusion.1
  152.2 3.9 copy.43
  156.1 4.9 copy.56
  161.0 4.9 copy.39
  165.9 4.0 add.26
  169.9 2.0 copy-done.5
  173.6 2.2 copy.40
  177.0 3.8 copy.44
  180.8 5.1 pad_maximum_fusion.1
  185.9 4.7 copy.45
  190.7 2.2 copy.41
  192.9 3.3 pad_maximum_fusion.4
  196.2 2.6 copy.46.h
  200.2 24.7 %shard_map.112 = (f32[32,384,128]{2,1,0:T(8,128)}, f32[16,384,128]{2,1,0:T(8,128)}) custom-call(s32[256]{0:T(256)S(1)} %bitcast.41, s32[1]{0:T(128)} %bitcast.34.count, bf16[16,384,128]{2,1,0:T(8,128)(2,1)S(1)} %copy-done.2, bf16[32,384,128]{2,1,0:T(8,128)(2,1)} %bitcast.47, bf16[256,128,128]{2,1,0:T(8,128)(2,1)} %bitcast.50), custom_call_target="tpu_custom_call" | custom-call | flops 6442450944 | bytes 33554432 | tf_op jit(solution)/shard_map/pallas_call | solution.py:132
  224.9 6.3 %fusion.2 = (f32[32,192,128]{2,1,0:T(8,128)}, f32[32,192,128]{2,1,0:T(8,128)}) fusion(f32[32,384,128]{2,1,0:T(8,128)} %get-tuple-element.6), kind=kLoop, calls=%fused_computation.22 | loop fusion | bytes 12582912 | tf_op jit(solution)/shard_map/slice | solution.py:216
  232.5 5.6 %collective-permute-done.4 = f32[32,192,128]{2,1,0:T(8,128)} collective-permute-done((f32[32,192,128]{2,1,0:T(8,128)}, f32[32,192,128]{2,1,0:T(8,128)}, u32[]{:S(2)}, u32[]{:S(2)}) %collective-permute-start.4) | collective-permute-done | bytes 3145760 | tf_op jit(solution)/shard_map/ppermute | solution.py:175
  238.2 7.5 %maximum_select_fusion = f32[64,192,128]{2,1,0:T(8,128)} fusion(f32[32,192,128]{2,1,0:T(8,128)} %collective-permute-done.4, f32[32,192,128]{2,1,0:T(8,128)} %get-tuple-element.24, pred[]{:T(512)S(6)} %eq.4), kind=kLoop, calls=%fused_computation | loop fusion | flops 4718592 | bytes 12582913 | tf_op jit(solution)/shard_map/jit(_where)/select_n | solution.py:217
  246.0 2.7 slice.37
  249.1 3.5 copy.48
  252.6 2.9 copy.49
  255.5 4.7 multiply_convert_fusion.1
  263.2 3.9 copy.50
  267.3 3.5 collective-permute-done.6
  270.9 3.7 copy.51
  274.6 4.4 pad_maximum_fusion.2
  278.9 4.6 copy.52.grads
  283.6 1.9 copy-done
  285.5 50.5 %shard_map.113 = f32[32,384,128]{2,1,0:T(8,128)} custom-call(s32[256]{0:T(256)S(1)} %bitcast.39, s32[1]{0:T(128)} %bitcast.32.count, bf16[16,384,256]{2,1,0:T(8,128)(2,1)S(1)} %copy-done, bf16[2,256,128,128]{3,2,1,0:T(8,128)(2,1)} %bitcast.44), custom_call_target="tpu_custom_call" | custom-call | flops 6442450944 | bytes 33554432 | tf_op jit(solution)/shard_map/pallas_call | solution.py:132
  336.0 3.3 fusion.1
  339.4 5.6 %collective-permute-done.7 = f32[32,192,128]{2,1,0:T(8,128)S(1)} collective-permute-done((f32[32,192,128]{2,1,0:T(8,128)S(1)}, f32[32,192,128]{2,1,0:T(8,128)S(1)}, u32[]{:S(2)}, u32[]{:S(2)}) %collective-permute-start.7) | collective-permute-done | bytes 3145760 | tf_op jit(solution)/shard_map/ppermute | solution.py:175
  345.1 3.2 maximum_select_fusion.1
  348.3 2.2 fusion.4.ht
  350.5 20.6 %shard_map.115 = f32[256,128,128]{2,1,0:T(8,128)} custom-call(s32[256]{0:T(256)S(1)} %bitcast.42, s32[1]{0:T(128)} %bitcast.35.count, bf16[16,128,384]{2,1,0:T(8,128)(2,1)S(1)} %fusion.4.ht, bf16[32,384,128]{2,1,0:T(8,128)(2,1)} %bitcast.48), custom_call_target="tpu_custom_call" | custom-call | flops 3221225472 | bytes 33554432 | tf_op jit(solution)/shard_map/pallas_call | solution.py:132
  371.2 47.5 %shard_map.114 = f32[2,256,128,128]{3,2,1,0:T(8,128)} custom-call(s32[256]{0:T(256)S(1)} %bitcast.40, s32[1]{0:T(128)} %bitcast.33.count, bf16[32,128,384]{2,1,0:T(8,128)(2,1)S(1)} %bitcast.37, bf16[16,384,256]{2,1,0:T(8,128)(2,1)} %copy.52.grads), custom_call_target="tpu_custom_call" | custom-call | flops 6442450944 | bytes 33554432 | tf_op jit(solution)/shard_map/pallas_call | solution.py:132
  418.7 1.9 copy_bitcast_fusion.1
  420.7 98.7 %reduce-scatter.5.cloned.1.call-done = f32[8,192,128]{2,1,0:T(8,128)} async-done(((f32[64,192,128]{2,1,0:T(8,128)}), f32[8,192,128]{2,1,0:T(8,128)}) %reduce-scatter.5.cloned.1.call-update) | async-done | bytes 786448 | tf_op jit(solution)/shard_map/reduce_scatter | solution.py:222
  519.4 1.9 copy_bitcast_fusion
  (36 shorter events, 9.8 us)
Async XLA Ops:
  7.2 66.3 %all-gather.3.cloned.1.call-start = ((), (), s32[]{:S(2)}) async-start(), calls=%async_computation.2 | async-start | bytes 3538944 | tf_op jit(solution)/shard_map/all_gather | solution.py:178
  7.9 139.8 %all-gather.5.cloned.1.call-start = ((), (), s32[]{:S(2)}) async-start(), calls=%async_computation.3 | async-start | bytes 4718592 | tf_op jit(solution)/shard_map/all_gather | solution.py:178
  10.0 408.7 %reduce-scatter.3.cloned.1.call-start = ((), (), s32[]{:S(2)}) async-start(), calls=%async_computation.4 | async-start | bytes 7077888 | tf_op jit(solution)/shard_map/reduce_scatter | solution.py:222
  75.6 3.5 collective-permute-start
  84.7 2.9 copy-start.3
  87.5 1.9 copy-start.1
  143.0 18.0 %collective-permute-start.1 = (f32[16,192,256]{2,1,0:T(8,128)}, f32[16,192,256]{2,1,0:T(8,128)}, u32[]{:S(2)}, u32[]{:S(2)}) collective-permute-start(f32[16,192,256]{2,1,0:T(8,128)} %get-tuple-element.26), channel_id=1, source_target_pairs={{0,1},{1,0},{2,3},{3,2},{4,5},{5,4},{6,7},{7,6},{8,9},{9,8},{10,11... | collective-permute-start | bytes 9437192 | tf_op jit(solution)/shard_map/ppermute | solution.py:175
  156.1 20.9 %collective-permute-start.3 = (bf16[192,4096]{1,0:T(8,128)(2,1)}, bf16[192,4096]{1,0:T(8,128)(2,1)}, u32[]{:S(2)}, u32[]{:S(2)}) collective-permute-start(bf16[192,4096]{1,0:T(8,128)(2,1)} %copy.43), channel_id=1, source_target_pairs={{0,1},{1,0},{2,3},{3,2},{4,5},{5,4},{6,7},{7,6},{8,9},{9,8},{10,11... | collective-permute-start | bytes 4718600 | tf_op jit(solution)/shard_map/ppermute | solution.py:175
  169.9 2.0 copy-start.5
  175.8 14.8 %collective-permute-start.2 = (bf16[16,192,128]{2,1,0:T(8,128)(2,1)}, bf16[16,192,128]{2,1,0:T(8,128)(2,1)}, u32[]{:S(2)}, u32[]{:S(2)}) collective-permute-start(bf16[16,192,128]{2,1,0:T(8,128)(2,1)} %copy.40), channel_id=1, source_target_pairs={{0,1},{1,0},{2,3},{3,2},{4,5},{5,4},{6,7},{7,6},{8,9},{9,8},{10,11... | collective-permute-start | bytes 2359304 | tf_op jit(solution)/shard_map/ppermute | solution.py:175
  192.9 5.9 %copy-start.4 = (s32[1,256]{1,0:T(1,128)S(1)}, s32[1,256]{1,0:T(1,128)}, u32[]{:S(2)}) copy-start(s32[1,256]{1,0:T(1,128)} %param.13) | copy-start | bytes 3076
  198.8 1.4 copy-start.2
  231.1 7.0 %collective-permute-start.4 = (f32[32,192,128]{2,1,0:T(8,128)}, f32[32,192,128]{2,1,0:T(8,128)}, u32[]{:S(2)}, u32[]{:S(2)}) collective-permute-start(f32[32,192,128]{2,1,0:T(8,128)} %get-tuple-element.25), channel_id=1, source_target_pairs={{0,1},{1,0},{2,3},{3,2},{4,5},{5,4},{6,7},{7,6},{8,9},{9,8},{10,11... | collective-permute-start | bytes 9437192 | tf_op jit(solution)/shard_map/ppermute | solution.py:175
  245.7 273.7 %reduce-scatter.5.cloned.1.call-start = ((), (), s32[]{:S(2)}) async-start(), calls=%async_computation.5 | async-start | bytes 7077888 | tf_op jit(solution)/shard_map/reduce_scatter | solution.py:222
  248.7 3.9 collective-permute-start.5
  260.2 1.0 copy-start.6
  260.2 1.3 copy-start.7
  267.1 3.8 collective-permute-start.6
  283.6 1.9 copy-start
  339.4 5.7 %collective-permute-start.7 = (f32[32,192,128]{2,1,0:T(8,128)S(1)}, f32[32,192,128]{2,1,0:T(8,128)S(1)}, u32[]{:S(2)}, u32[]{:S(2)}) collective-permute-start(f32[32,192,128]{2,1,0:T(8,128)S(1)} %get-tuple-element.23), channel_id=1, source_target_pairs={{0,1},{1,0},{2,3},{3,2},{4,5},{5,4},{6,7},{7,6},{8,9},{9,8},{10,11... | collective-permute-start | bytes 9437192 | tf_op jit(solution)/shard_map/ppermute | solution.py:175
Sparse Core Ops, SparseCore 0:
  10.2 63.1 all-gather.2
  75.5 72.0 all-gather.4
  245.8 152.9 reduce-scatter.2
  402.3 117.0 reduce-scatter.4
